TPU v7x, 32 devices: a whole 2x2x4 slice. The times are simulated.
32 devices in a mesh: rep: 2 (over y), wide: 8 (over z, x), narrow: 2 (over core).
Axes of the slice: x: 2, y: 2, z: 4, core: 2. Of those that a mesh axis runs over, the one named last changes fastest.
Arguments:
- hidden_rows: bfloat16 [128, 16384], P(('rep', 'wide'), 'narrow'), parts along dimension 0, may hold values from -600 to 600, as said below
- query_weight: bfloat16 [16384, 16384], P('narrow', 'wide'), may hold values from -0.046875 to 0.046875
- key_value_weight: bfloat16 [16384, 2048], P('narrow', 'wide'), may hold values from -0.046875 to 0.046875
- cache_keys: bfloat16 [128, 192, 1024], P(('rep', 'wide', 'narrow')), parts along dimension 0, may hold values from -200 to 200, as said below
- earlier_values: bfloat16 [128, 192, 1024], P(('rep', 'wide', 'narrow')), parts along dimension 0, may hold values from -6 to 6
- lengths: int32 [128], P(('rep', 'wide', 'narrow')), parts along dimension 0, may hold values from 1 to 192, as said below
- positions: int32 [128], P(('rep', 'wide', 'narrow')), parts along dimension 0, may hold values from 0 to 8191
Outputs:
- attended: bfloat16 [128, 16384], P(('rep', 'wide', 'narrow')), parts along dimension 0
There are 2 independent parts, one for each index of `rep`. A program takes and returns all parts, laid end to end along the dimension named above; an argument that names none is the same for every part. Nothing has to cross between parts.
Inputs may be any that keep to these rules, and one draw needn't show every extreme that they name: `hidden_rows`: entries are finite. `cache_keys`: entries are finite. `lengths`: some row has all 192 slots live.
All inputs are finite; a program needn't handle non-finite values.
Results may differ from a plain program's by a relative error of at most 0.00455.
The roundings to bfloat16 on the way count: a program that leaves them out, or rounds other values in their place, can miss the bound.
Values may be sent and summed in bfloat16 or wider, within the bound.
A program may use at most 128 MiB of HBM per device.

v0:
```python
import jax
import jax.numpy as jnp
from jax import lax
from jax.sharding import PartitionSpec as P

MODEL_WIDTH = 16384
HEAD_WIDTH = 128


EPSILON = 1e-05


def rotate(values, positions):
    middle = values.shape[-1] // 2
    frequency = 500000.0 ** (-(jnp.arange(middle).astype(jnp.float32) * 2.0 / values.shape[-1]))
    angles = positions.astype(jnp.float32)[:, None] * frequency[None, :]
    cosine = jnp.cos(angles)[:, None, :]
    sine_part = jnp.sin(angles)[:, None, :]
    leading = values[..., :middle]
    trailing = values[..., middle:]
    return jnp.concatenate(
        [leading * cosine - trailing * sine_part, trailing * cosine + leading * sine_part], axis=-1
    )


def attend(queries, new_pair, cached_keys, cached_values, lengths, positions):
    row_count, head_count, head_size = queries.shape
    kv_heads = cached_keys.shape[-1] // head_size
    group_size = head_count // kv_heads
    rotated = rotate(queries.astype(jnp.float32), positions).astype(jnp.bfloat16)
    split_pair = new_pair.reshape(row_count, kv_heads, 2, head_size)
    new_key = rotate(split_pair[:, :, 0, :].astype(jnp.float32), positions).astype(jnp.bfloat16)
    new_value = split_pair[:, :, 1, :]
    grouped = rotated.reshape(row_count, kv_heads, group_size, head_size)
    key_blocks = cached_keys.reshape(row_count, -1, kv_heads, head_size)
    value_blocks = cached_values.reshape(row_count, -1, kv_heads, head_size)
    scaling = head_size ** (-0.5)
    scores = (
        jnp.einsum("rhgd,rchd->rhgc", grouped, key_blocks, preferred_element_type=jnp.float32)
        * scaling
    )
    own_score = (
        jnp.einsum("rhgd,rhd->rhg", grouped, new_key, preferred_element_type=jnp.float32) * scaling
    )
    live_mask = (jnp.arange(key_blocks.shape[1])[None, :] < lengths[:, None])[:, None, None, :]
    masked = jnp.where(live_mask, scores, -1e30)
    peak_score = jnp.maximum(jnp.max(masked, axis=-1), own_score)
    weights = jnp.where(live_mask, jnp.exp(masked - peak_score[..., None]), 0.0)
    own_weight = jnp.exp(own_score - peak_score)
    totals = jnp.sum(weights, axis=-1) + own_weight
    rounded = weights.astype(jnp.bfloat16)
    own_rounded = own_weight.astype(jnp.bfloat16).astype(jnp.float32)
    blended = jnp.einsum(
        "rhgc,rchd->rhgd", rounded, value_blocks, preferred_element_type=jnp.float32
    )
    blended = blended + own_rounded[..., None] * new_value.astype(jnp.float32)[:, :, None, :]
    return (
        (blended / totals[..., None])
        .reshape(row_count, head_count * head_size)
        .astype(jnp.bfloat16)
    )


def shards(
    hidden_rows, query_weight, key_value_weight, cache_keys, earlier_values, lengths, positions
):
    wide_count = lax.axis_size("wide")
    narrow_count = lax.axis_size("narrow")
    query_cols = query_weight.shape[1]
    gathered = lax.all_gather(hidden_rows, "wide", axis=0, tiled=True)
    widened = gathered.astype(jnp.float32)
    squares = lax.psum(jnp.sum(widened * widened, axis=1), "narrow")
    normed = (widened * lax.rsqrt(squares / MODEL_WIDTH + EPSILON)[:, None]).astype(jnp.bfloat16)
    query_part = jnp.dot(normed, query_weight, preferred_element_type=jnp.float32)
    pair_part = jnp.dot(normed, key_value_weight, preferred_element_type=jnp.float32)
    row_each = query_part.shape[0] // (wide_count * narrow_count)
    shaped_query = query_part.reshape(wide_count, narrow_count, row_each, 1, query_cols)
    shaped_pair = pair_part.reshape(
        wide_count, narrow_count, row_each, 1, key_value_weight.shape[1]
    )
    summed_query, summed_pair = (
        lax.psum_scatter(shaped_query, "narrow", scatter_dimension=1, tiled=True),
        lax.psum_scatter(shaped_pair, "narrow", scatter_dimension=1, tiled=True),
    )
    moved_query, moved_pair = (
        lax.all_to_all(
            summed_query.astype(jnp.bfloat16), "wide", split_axis=0, concat_axis=3, tiled=True
        ),
        lax.all_to_all(
            summed_pair.astype(jnp.bfloat16), "wide", split_axis=0, concat_axis=3, tiled=True
        ),
    )
    queries = moved_query.reshape(row_each, -1, HEAD_WIDTH)
    new_pair = moved_pair.reshape(row_each, -1)
    return attend(queries, new_pair, cache_keys, earlier_values, lengths, positions)


def solution(mesh):
    in_specs = (
        P(("rep", "wide"), "narrow"),
        P("narrow", "wide"),
        P("narrow", "wide"),
        P(("rep", "wide", "narrow"), None, None),
        P(("rep", "wide", "narrow"), None, None),
        P(("rep", "wide", "narrow")),
        P(("rep", "wide", "narrow")),
    )
    out_specs = P(("rep", "wide", "narrow"), None)
    return jax.shard_map(shards, mesh=mesh, in_specs=in_specs, out_specs=out_specs, check_vma=False)
```

profile of v0, /device:TPU:0, one launch (start us, length us, event | category | flops | bytes accessed | tf_op | source)
XLA Modules:
  0.0 109.6 jit_solution(11664597539553565707)
XLA Ops:
  6.5 0.0 copy-start
  6.5 0.0 all-gather.2.cloned.1.call-start
  6.5 0.7 all-gather.2.cloned.1.call-update
  7.3 0.0 reduce-scatter.5.cloned.1.call-start
  7.3 45.1 %all-gather.2.cloned.1.call-done = bf16[64,8192]{1,0:T(8,128)(2,1)} async-done(((bf16[8,8192]{1,0:T(8,128)(2,1)}), bf16[64,8192]{1,0:T(8,128)(2,1)}) %all-gather.2.cloned.1.call-update) | async-done | bytes 1048592 | tf_op jit(solution)/shard_map/all_gather | solution.py:70
  52.4 1.5 %fusion = f32[64]{0:T(128)S(1)} fusion(bf16[64,8192]{1,0:T(8,128)(2,1)} %all-gather.2.cloned.1.call-done), kind=kLoop, calls=%fused_computation.2 | loop fusion | flops 1572800 | bytes 1048832 | tf_op jit(solution)/shard_map/reduce_sum | solution.py:72
  53.9 2.5 %psum.7 = f32[64]{0:T(128)S(1)} all-reduce(f32[64]{0:T(128)S(1)} %fusion), channel_id=1, replica_groups=mesh['rep'=2,'wide'=8,'narrow'=2] {'narrow'}, use_global_device_ids=true, to_apply=%region_1.0 | all-reduce | flops 64 | bytes 512 | tf_op jit(solution)/shard_map/psum | solution.py:72
  56.4 0.0 copy-start.1
  56.4 3.5 %fusion.25 = f32[64,256]{1,0:T(8,128)S(1)} fusion(bf16[8192,256]{1,0:T(8,128)(2,1)} %param.9, bf16[64,8192]{1,0:T(8,128)(2,1)} %all-gather.2.cloned.1.call-done, f32[64]{0:T(128)S(1)} %add_rsqrt_fusion), kind=kOutput, calls=%fused_computation.18 | convolution fusion | flops 270008320 | bytes 5308672 | tf_op jit(solution)/shard_map/dot_general | solution.py:75
  59.9 0.7 copy.26
  60.6 0.0 reduce-scatter.5.cloned.1.call-update
  60.6 0.0 reduce-scatter.3.cloned.1.call-start
  60.6 0.0 copy-done.1
  60.6 13.7 %fusion.27 = f32[64,2048]{1,0:T(8,128)S(1)} fusion(bf16[8192,2048]{1,0:T(8,128)(2,1)} %param.8, bf16[64,8192]{1,0:T(8,128)(2,1)S(1)} %copy-done.1, f32[64]{0:T(128)S(1)} %add_rsqrt_fusion), kind=kOutput, calls=%fused_computation.19 | convolution fusion | flops 2149056512 | bytes 35127552 | tf_op jit(solution)/shard_map/dot_general | solution.py:74
  74.4 0.0 copy-start.3
  74.4 0.0 copy-start.4
  74.4 0.1 reshape.101
  74.5 1.1 %copy.22 = f32[8,2,4,1,2048]{4,0,3,2,1:T(8,128)} copy(f32[8,2,4,1,2048]{4,2,1,0,3:T(4,128)S(1)} %reshape.101) | data formatting | bytes 1048576 | tf_op jit(solution)/shard_map/reshape | solution.py:77
  75.6 0.0 reduce-scatter.3.cloned.1.call-update
  75.7 0.0 copy-done.3
  75.7 0.1 multiply_cosine_fusion
  75.8 0.0 reduce-scatter.5.cloned.1.call-done
  75.8 0.8 convert_element_type.71
  76.6 0.6 copy.27
  77.2 3.4 %all-to-all-start.1 = ((bf16[8,1,4,1,256]{4,2,1,3,0:T(4,128)(2,1)}), bf16[8,1,4,1,256]{4,2,1,3,0:T(4,128)(2,1)S(1)}, u32[]{:S(2)}, u32[]{:S(2)}) async-start(bf16[8,1,4,1,256]{4,2,1,3,0:T(4,128)(2,1)} %copy.27), calls=%async_computation.3 | async-start | bytes 32768 | tf_op jit(solution)/shard_map/all_to_all | solution.py:89
  80.6 0.0 copy-done.4
  80.6 0.1 iota_compare_fusion
  80.6 6.5 %all-to-all-done.1 = bf16[8,1,4,1,256]{4,2,1,3,0:T(4,128)(2,1)S(1)} async-done(((bf16[8,1,4,1,256]{4,2,1,3,0:T(4,128)(2,1)}), bf16[8,1,4,1,256]{4,2,1,3,0:T(4,128)(2,1)S(1)}, u32[]{:S(2)}, u32[]{:S(2)}) %all-to-all-start.1) | async-done | bytes 16416 | tf_op jit(solution)/shard_map/all_to_all | solution.py:89
  87.2 0.1 subtract_convert_fusion.1
  87.3 0.0 reduce-scatter.3.cloned.1.call-done
  87.3 1.0 convert_element_type.64
  88.3 0.8 copy.23
  89.0 3.4 %all-to-all-start = ((bf16[8,1,4,1,2048]{4,2,3,1,0:T(4,128)(2,1)}), bf16[8,1,4,1,2048]{4,2,3,1,0:T(4,128)(2,1)S(1)}, u32[]{:S(2)}, u32[]{:S(2)}) async-start(bf16[8,1,4,1,2048]{4,2,3,1,0:T(4,128)(2,1)} %copy.23), calls=%async_computation.1 | async-start | bytes 262144 | tf_op jit(solution)/shard_map/all_to_all | solution.py:86
  92.4 0.1 maximum_bitcast_fusion
  92.5 7.2 %all-to-all-done = bf16[8,1,4,1,2048]{4,2,3,1,0:T(4,128)(2,1)S(1)} async-done(((bf16[8,1,4,1,2048]{4,2,3,1,0:T(4,128)(2,1)}), bf16[8,1,4,1,2048]{4,2,3,1,0:T(4,128)(2,1)S(1)}, u32[]{:S(2)}, u32[]{:S(2)}) %all-to-all-start) | async-done | bytes 131104 | tf_op jit(solution)/shard_map/all_to_all | solution.py:86
  99.7 0.2 copy.24
  99.9 0.0 copy-start.2
  100.0 0.1 subtract_convert_fusion
  100.1 0.2 fusion.33
  100.4 0.0 copy-done
  100.4 1.0 fusion.41
  101.4 0.3 fusion.23
  101.7 0.0 copy-done.2
  101.7 0.6 fusion.20
  102.3 0.8 copy.62
  (11 shorter events, 0.2 us)
Async XLA Ops:
  6.5 93.8 %copy-start = (bf16[4,192,1024]{2,1,0:T(8,128)(2,1)S(1)}, bf16[4,192,1024]{2,1,0:T(8,128)(2,1)}, u32[]{:S(2)}) copy-start(bf16[4,192,1024]{2,1,0:T(8,128)(2,1)} %param.10) | copy-start | bytes 4718596
  6.5 45.8 %all-gather.2.cloned.1.call-start = ((), (), s32[]{:S(2)}) async-start(), calls=%async_computation.4 | async-start | bytes 1179648 | tf_op jit(solution)/shard_map/all_gather | solution.py:70
  7.3 68.6 %reduce-scatter.5.cloned.1.call-start = ((), (), s32[]{:S(2)}) async-start(), calls=%async_computation.6 | async-start | bytes 98304 | tf_op jit(solution)/shard_map/reduce_scatter | solution.py:83
  56.4 4.2 %copy-start.1 = (bf16[64,8192]{1,0:T(8,128)(2,1)S(1)}, bf16[64,8192]{1,0:T(8,128)(2,1)}, u32[]{:S(2)}) copy-start(bf16[64,8192]{1,0:T(8,128)(2,1)} %all-gather.2.cloned.1.call-done) | copy-start | bytes 3145732
  60.6 26.7 %reduce-scatter.3.cloned.1.call-start = ((), (), s32[]{:S(2)}) async-start(), calls=%async_computation.5 | async-start | bytes 786432 | tf_op jit(solution)/shard_map/reduce_scatter | solution.py:82
  74.4 1.3 %copy-start.3 = (s32[4]{0:T(128)S(1)}, s32[4]{0:T(128)}, u32[]{:S(2)}) copy-start(s32[4]{0:T(128)} %param.13) | copy-start | bytes 52
  74.4 6.2 %copy-start.4 = (s32[4]{0:T(128)S(1)}, s32[4]{0:T(128)}, u32[]{:S(2)}) copy-start(s32[4]{0:T(128)} %param.12) | copy-start | bytes 52
  77.2 9.9 %all-to-all-start.1 = ((bf16[8,1,4,1,256]{4,2,1,3,0:T(4,128)(2,1)}), bf16[8,1,4,1,256]{4,2,1,3,0:T(4,128)(2,1)S(1)}, u32[]{:S(2)}, u32[]{:S(2)}) async-start(bf16[8,1,4,1,256]{4,2,1,3,0:T(4,128)(2,1)} %copy.27), calls=%async_computation.3 | async-start | bytes 32768 | tf_op jit(solution)/shard_map/all_to_all | solution.py:89
  89.0 10.7 %all-to-all-start = ((bf16[8,1,4,1,2048]{4,2,3,1,0:T(4,128)(2,1)}), bf16[8,1,4,1,2048]{4,2,3,1,0:T(4,128)(2,1)S(1)}, u32[]{:S(2)}, u32[]{:S(2)}) async-start(bf16[8,1,4,1,2048]{4,2,3,1,0:T(4,128)(2,1)} %copy.23), calls=%async_computation.1 | async-start | bytes 262144 | tf_op jit(solution)/shard_map/all_to_all | solution.py:86
  99.9 1.8 %copy-start.2 = (bf16[4,192,1024]{2,1,0:T(8,128)(2,1)S(1)}, bf16[4,192,1024]{2,1,0:T(8,128)(2,1)}, u32[]{:S(2)}) copy-start(bf16[4,192,1024]{2,1,0:T(8,128)(2,1)} %param.11) | copy-start | bytes 4718596
Sparse Core Ops, SparseCore 0:
  9.5 42.8 all-gather.1
  60.7 6.2 reduce-scatter.4
  75.8 6.7 reduce-scatter.2
where the time goes:
time: 110 us
  waiting for transfers between devices  59.5 us (54%)
  matrix products  19.1 us (17%)
  between operations  13.3 us (12%)
  starting transfers between devices  6.81 us (6%)
  local copies, waits for them, and re-layouts  4.31 us (4%)
  other arithmetic  4.11 us (4%)
  blocking collectives  2.47 us (2%)
    all_gather x1, waiting for transfers between devices, shards(): gathered = lax.all_gather(hidden_rows, 'wide', axis=0, tiled=True)  45.1 us
    dot_general x1, matrix products, shards(): jnp.dot(normed, query_weight, preferred_element_type=jnp.float32)  13.7 us
    all_to_all x1, waiting for transfers between devices, shards(): lax.all_to_all(summed_query.astype(jnp.bfloat16), 'wide', split_axis=0, c...  7.19 us
    all_to_all x1, waiting for transfers between devices, shards(): lax.all_to_all(summed_pair.astype(jnp.bfloat16), 'wide', split_axis=0, co...  6.5 us
    dot_general x1, matrix products, shards(): jnp.dot(normed, key_value_weight, preferred_element_type=jnp.float32)  3.48 us
    all_to_all x1, starting transfers between devices, shards(): lax.all_to_all(summed_query.astype(jnp.bfloat16), 'wide', split_axis=0, c...  3.37 us
    all_to_all x1, starting transfers between devices, shards(): lax.all_to_all(summed_pair.astype(jnp.bfloat16), 'wide', split_axis=0, co...  3.36 us
    psum x1, blocking collectives, shards(): squares = lax.psum(jnp.sum(widened * widened, axis=1), 'narrow')  2.47 us
  transfers between devices with their start and end apart: 5, of which 3 were waited for; matrix products, arithmetic and copies ran while one was open for 15% of the time, Pallas kernels for 0%

commit v1 on v0

--- a/solution.py
+++ b/solution.py
@@ -1,6 +1,11 @@
+import functools
+
 import jax
 import jax.numpy as jnp
+import numpy as np
 from jax import lax
+from jax.experimental import pallas as pl
+from jax.experimental.pallas import tpu as pltpu
 from jax.sharding import PartitionSpec as P
 
 MODEL_WIDTH = 16384
@@ -95,7 +100,258 @@
     return attend(queries, new_pair, cache_keys, earlier_values, lengths, positions)
 
 
+WIDE = 8
+GROUP = 16
+HEADS = GROUP + 2
+CHUNKS = 4
+ROWS = 4
+SLOTS = 192
+PACK = 80
+MESH = pl.DeviceIdType.MESH
+
+
+def kernel(
+    x_ref, wq_ref, wkv_ref, keys_ref, values_ref, lengths_ref, positions_ref, freq_ref, out_ref,
+    gathered, wq, wkv, keys, values, left, acc, give, take, spread, parcel, landed, sums,
+    sum_send, sum_recv, own_send, fwd_send, gather_recv, wq_sem, wkv_sem, key_sem, value_sem,
+    give_send, give_recv, parcel_send, parcel_recv,
+):
+    me = lax.axis_index("wide")
+    core = lax.axis_index("narrow")
+    other = 1 - core
+    peer = me + 1 - 2 * lax.rem(me, 2)
+    features = x_ref.shape[1]
+    width = features // CHUNKS
+    half = width // 2
+
+    def wq_copy(c):
+        return pltpu.make_async_copy(wq_ref.at[pl.ds(c * width, width)], wq.at[c], wq_sem.at[c])
+
+    def wkv_copy(c):
+        return pltpu.make_async_copy(wkv_ref.at[pl.ds(c * width, width)], wkv.at[c], wkv_sem.at[c])
+
+    key_copy = pltpu.make_async_copy(keys_ref, keys, key_sem)
+    value_copy = pltpu.make_async_copy(values_ref, values, value_sem)
+
+    barrier = pltpu.get_barrier_semaphore()
+    for d in range(1, WIDE):
+        pl.semaphore_signal(
+            barrier, inc=1, device_id={"wide": lax.rem(me + d, WIDE)}, device_id_type=MESH
+        )
+    pl.semaphore_signal(barrier, inc=1, device_id={"narrow": other}, device_id_type=MESH)
+
+    for c in range(CHUNKS):
+        wq_copy(c).start()
+        wkv_copy(c).start()
+    key_copy.start()
+    value_copy.start()
+
+    widened = x_ref[...].astype(jnp.float32)
+    mine = jnp.sum(widened * widened, axis=1, keepdims=True)
+    sums[0] = jnp.broadcast_to(mine, (8, 128))
+    pl.semaphore_wait(barrier, WIDE)
+    swap = pltpu.make_async_remote_copy(
+        src_ref=sums.at[0], dst_ref=sums.at[1], send_sem=sum_send, recv_sem=sum_recv,
+        device_id={"narrow": other}, device_id_type=MESH,
+    )
+    swap.start()
+    swap.wait()
+    squares = sums[0] + sums[1]
+    scale = lax.rsqrt(squares / MODEL_WIDTH + EPSILON)[:, :1]
+
+    def send(c, slot, target, sem):
+        return pltpu.make_async_remote_copy(
+            src_ref=gathered.at[c, slot], dst_ref=gathered.at[c, slot], send_sem=sem,
+            recv_sem=gather_recv.at[c, slot], device_id={"wide": target}, device_id_type=MESH,
+        )
+
+    def along(c, d):
+        return send(c, me, lax.rem(me + 2 * d, WIDE), own_send.at[c, d])
+
+    def across(c):
+        return send(c, me, peer, own_send.at[c, 0])
+
+    def forward(c, d):
+        return send(c, lax.rem(me + 2 * d, WIDE), peer, fwd_send.at[c, d])
+
+    for c in range(CHUNKS):
+        first = x_ref[:, c * width : c * width + half].astype(jnp.float32) * scale
+        second = x_ref[:, c * width + half : (c + 1) * width].astype(jnp.float32) * scale
+        gathered[c, me] = jnp.concatenate([first, second], axis=0).astype(jnp.bfloat16)
+        for d in range(1, 4):
+            along(c, d).start()
+        across(c).start()
+
+    angles = [positions_ref[r].astype(jnp.float32) * freq_ref[0:1, :] for r in range(ROWS)]
+    cosine = [jnp.cos(a) for a in angles]
+    sign = jnp.where(lax.broadcasted_iota(jnp.int32, (1, HEAD_WIDTH), 1) < HEAD_WIDTH // 2, -1.0, 1.0)
+    sine = [jnp.sin(a) * sign for a in angles]
+
+    def pass_on(c):
+        for d in (1, 3, 2):
+            slot = lax.rem(me + 2 * d, WIDE)
+            send(c, slot, peer, fwd_send.at[c, d]).wait_recv()
+            forward(c, d).start()
+
+    pass_on(0)
+    for c in range(CHUNKS):
+        if c + 1 < CHUNKS:
+            pass_on(c + 1)
+        for d in range(4):
+            slot = lax.rem(peer + 2 * d, WIDE)
+            send(c, slot, peer, fwd_send.at[c, 0]).wait_recv()
+        block = gathered[c].astype(jnp.float32)
+        left[:, :half] = block[:, :8].reshape(8 * WIDE, half).astype(jnp.bfloat16)
+        left[:, half:] = block[:, 8:].reshape(8 * WIDE, half).astype(jnp.bfloat16)
+        wq_copy(c).wait()
+        wkv_copy(c).wait()
+
+        def accumulate(j, product):
+            for i in range(2):
+                at = pl.ds(pl.multiple_of((2 * j + i) * 64, 64), 64)
+                piece = product[:, i * 128 : (i + 1) * 128]
+                if c == 0:
+                    acc[at, :] = piece
+                else:
+                    acc[at, :] += piece
+
+        def tile(j, carry):
+            columns = pl.ds(pl.multiple_of(j * 256, 256), 256)
+            accumulate(
+                j, jnp.dot(left[...], wq[c, :, columns], preferred_element_type=jnp.float32)
+            )
+            return carry
+
+        lax.fori_loop(0, GROUP // 2, tile, 0)
+        accumulate(
+            GROUP // 2, jnp.dot(left[...], wkv[c], preferred_element_type=jnp.float32)
+        )
+
+    for h in range(HEADS):
+        for r in range(ROWS):
+            give[pl.ds(h * 32 + r * 8, 8), :] = acc[pl.ds(h * 64 + other * 4 + r, 8, stride=8), :]
+    trade = pltpu.make_async_remote_copy(
+        src_ref=give, dst_ref=take, send_sem=give_send, recv_sem=give_recv,
+        device_id={"narrow": other}, device_id_type=MESH,
+    )
+    trade.start()
+    for w in range(WIDE):
+        spread[pl.ds(w * PACK + 72, 8), :] = jnp.zeros((8, HEAD_WIDTH), jnp.float32)
+    trade.wait()
+    for h in range(HEADS):
+        for r in range(ROWS):
+            total = (
+                acc[pl.ds(h * 64 + core * 4 + r, 8, stride=8), :]
+                + take[pl.ds(h * 32 + r * 8, 8), :]
+            )
+            row = r * GROUP + h if h < GROUP else 64 + 2 * r + h - GROUP
+            spread[pl.ds(row, 8, stride=PACK), :] = total
+
+    def deliver(d):
+        target = lax.rem(me + d, WIDE)
+        return pltpu.make_async_remote_copy(
+            src_ref=parcel.at[target], dst_ref=landed.at[me], send_sem=parcel_send.at[target],
+            recv_sem=parcel_recv.at[me], device_id={"wide": target}, device_id_type=MESH,
+        )
+
+    parcel[...] = spread[...].astype(jnp.bfloat16).reshape(WIDE, PACK, HEAD_WIDTH)
+    for d in (4, 3, 5, 2, 6, 1, 7):
+        deliver(d).start()
+    landed[me] = parcel[me]
+    key_copy.wait()
+    value_copy.wait()
+    for d in range(1, WIDE):
+        source = lax.rem(me + d, WIDE)
+        pltpu.make_async_remote_copy(
+            src_ref=parcel.at[source], dst_ref=landed.at[source], send_sem=parcel_send.at[source],
+            recv_sem=parcel_recv.at[source], device_id={"wide": source}, device_id_type=MESH,
+        ).wait_recv()
+
+    scaling = HEAD_WIDTH ** (-0.5)
+    slot_index = lax.broadcasted_iota(jnp.int32, (GROUP, SLOTS), 1)
+
+    def rotated(v, r):
+        return (v * cosine[r] + pltpu.roll(v, HEAD_WIDTH // 2, 1) * sine[r]).astype(jnp.bfloat16)
+
+    for r in range(ROWS):
+        live = slot_index < lengths_ref[r]
+        for g in range(WIDE):
+            columns = slice(g * HEAD_WIDTH, (g + 1) * HEAD_WIDTH)
+            query = rotated(landed[g, r * GROUP : (r + 1) * GROUP, :].astype(jnp.float32), r)
+            pair = landed[g, 64:PACK, :].astype(jnp.float32)
+            new_key = rotated(pair, r)[2 * r : 2 * r + 1].astype(jnp.float32)
+            new_value = pair[2 * r + 1 : 2 * r + 2]
+            own = jnp.sum(query.astype(jnp.float32) * new_key, axis=1, keepdims=True) * scaling
+            scores = lax.dot_general(
+                query, keys[r, :, columns], (((1,), (1,)), ((), ())),
+                preferred_element_type=jnp.float32,
+            ) * scaling
+            masked = jnp.where(live, scores, -1e30)
+            peak = jnp.maximum(jnp.max(masked, axis=1, keepdims=True), own)
+            weights = jnp.where(live, jnp.exp(masked - peak), 0.0)
+            own_weight = jnp.exp(own - peak)
+            totals = jnp.sum(weights, axis=1, keepdims=True) + own_weight
+            blended = jnp.dot(
+                weights.astype(jnp.bfloat16), values[r, :, columns],
+                preferred_element_type=jnp.float32,
+            )
+            blended = blended + own_weight.astype(jnp.bfloat16).astype(jnp.float32) * new_value
+            at = r * WIDE * GROUP + g * GROUP
+            out_ref[at : at + GROUP, :] = (blended / totals).astype(jnp.bfloat16)
+
+    for c in range(CHUNKS):
+        for d in range(1, 4):
+            along(c, d).wait_send()
+            forward(c, d).wait_send()
+        across(c).wait_send()
+    for d in range(1, WIDE):
+        deliver(d).wait_send()
+
+
+def fused(
+    hidden_rows, query_weight, key_value_weight, cache_keys, earlier_values, lengths, positions
+):
+    features = hidden_rows.shape[1]
+    width = features // CHUNKS
+    frequency = 500000.0 ** (-(jnp.arange(HEAD_WIDTH // 2).astype(jnp.float32) * 2.0 / HEAD_WIDTH))
+    frequency = jnp.broadcast_to(jnp.concatenate([frequency, frequency])[None], (8, HEAD_WIDTH))
+    dma = pltpu.SemaphoreType.DMA
+    vmem, anywhere, smem = (pl.BlockSpec(memory_space=s) for s in (pltpu.VMEM, pl.ANY, pltpu.SMEM))
+    result = pl.pallas_call(
+        kernel,
+        out_shape=jax.ShapeDtypeStruct((ROWS * WIDE * GROUP, HEAD_WIDTH), jnp.bfloat16),
+        in_specs=[vmem, anywhere, anywhere, anywhere, anywhere, smem, smem, vmem],
+        out_specs=vmem,
+        scratch_shapes=[
+            pltpu.VMEM((CHUNKS, WIDE, 16, width // 2), jnp.bfloat16),
+            pltpu.VMEM((CHUNKS, width, GROUP * HEAD_WIDTH), jnp.bfloat16),
+            pltpu.VMEM((CHUNKS, width, 2 * HEAD_WIDTH), jnp.bfloat16),
+            pltpu.VMEM((ROWS, SLOTS, WIDE * HEAD_WIDTH), jnp.bfloat16),
+            pltpu.VMEM((ROWS, SLOTS, WIDE * HEAD_WIDTH), jnp.bfloat16),
+            pltpu.VMEM((8 * WIDE, width), jnp.bfloat16),
+            pltpu.VMEM((HEADS * 64, HEAD_WIDTH), jnp.float32),
+            pltpu.VMEM((HEADS * 32, HEAD_WIDTH), jnp.float32),
+            pltpu.VMEM((HEADS * 32, HEAD_WIDTH), jnp.float32),
+            pltpu.VMEM((WIDE * PACK, HEAD_WIDTH), jnp.float32),
+            pltpu.VMEM((WIDE, PACK, HEAD_WIDTH), jnp.bfloat16),
+            pltpu.VMEM((WIDE, PACK, HEAD_WIDTH), jnp.bfloat16),
+            pltpu.VMEM((2, 8, 128), jnp.float32),
+            dma, dma, dma((CHUNKS, 4)), dma((CHUNKS, 4)), dma((CHUNKS, WIDE)),
+            dma((CHUNKS,)), dma((CHUNKS,)), dma, dma,
+            dma, dma, dma((WIDE,)), dma((WIDE,)),
+        ],
+        compiler_params=pltpu.CompilerParams(
+            collective_id=0, has_side_effects=True, vmem_limit_bytes=56 * 1024 * 1024
+        ),
+    )(
+        hidden_rows, query_weight, key_value_weight, cache_keys, earlier_values, lengths,
+        positions, frequency,
+    )
+    return result.reshape(ROWS, WIDE * GROUP * HEAD_WIDTH)
+
+
 def solution(mesh):
+    body = fused if mesh.shape["wide"] == WIDE and mesh.shape["narrow"] == 2 else shards
     in_specs = (
         P(("rep", "wide"), "narrow"),
         P("narrow", "wide"),
@@ -106,4 +362,4 @@
         P(("rep", "wide", "narrow")),
     )
     out_specs = P(("rep", "wide", "narrow"), None)
-    return jax.shard_map(shards, mesh=mesh, in_specs=in_specs, out_specs=out_specs, check_vma=False)
+    return jax.shard_map(body, mesh=mesh, in_specs=in_specs, out_specs=out_specs, check_vma=False)

time: 110 us -> 49.3 us (0.45)
  waiting for transfers between devices: 59.5 us -> 0 us
  Pallas kernels: 0 us -> 46.8 us
  matrix products: 19.1 us -> 0 us
  between operations: 13.3 us -> 0.01 us
  starting transfers between devices: 6.81 us -> 0 us
  other arithmetic: 4.11 us -> 0.08 us
  blocking collectives: 2.47 us -> 0 us
  local copies, waits for them, and re-layouts: 4.31 us -> 2.21 us
    pallas_call x0 -> x1, Pallas kernels: none -> 46.8 us  [fused(): pl.pallas_call(kernel, out_shape=jax.ShapeDtypeStruct((ROWS * WIDE * GROU...]
    all_gather x1 -> x0, waiting for transfers between devices: 45.1 us -> none  [shards(): gathered = lax.all_gather(hidden_rows, 'wide', axis=0, tiled=True)]
    dot_general x5 -> x0, matrix products: 19.1 us -> none  [the longest x1 13.7 us: shards(): jnp.dot(normed, query_weight, preferred_element_type=jnp.float32)]
    all_to_all x2 -> x0, waiting for transfers between devices: 13.7 us -> none  [the longest x1 7.19 us: shards(): lax.all_to_all(summed_query.astype(jnp.bfloat16), 'wide', split_axis=0, c...]
    all_to_all x2 -> x0, starting transfers between devices: 6.73 us -> none  [the longest x1 3.37 us: shards(): lax.all_to_all(summed_query.astype(jnp.bfloat16), 'wide', split_axis=0, c...]
    psum x1 -> x0, blocking collectives: 2.47 us -> none  [shards(): squares = lax.psum(jnp.sum(widened * widened, axis=1), 'narrow')]
    reduce_sum x2 -> x0, other arithmetic: 1.79 us -> none  [the longest x1 1.53 us: shards(): squares = lax.psum(jnp.sum(widened * widened, axis=1), 'narrow')]
    convert_element_type x5 -> x0, other arithmetic: 1.76 us -> none  [the longest x1 0.97 us: shards(): summed_query.astype(jnp.bfloat16)]
  transfers between devices with their start and end apart: 5 -> 0, of which waited for: 3 -> 0; matrix products, arithmetic and copies ran while one was open for 15% -> 0% of each run, Pallas kernels for 0% -> 0%
where the time goes in v1:
time: 49.3 us; the launch traced here: 49.1 us
  Pallas kernels  46.8 us (95%)
  local copies, waits for them, and re-layouts  2.21 us (4%)
    pallas_call x1, Pallas kernels, fused(): pl.pallas_call(kernel, out_shape=jax.ShapeDtypeStruct((ROWS * WIDE * GROU...  46.8 us
    reshape x1, local copies, waits for them, and re-layouts, fused(): return result.reshape(ROWS, WIDE * GROUP * HEAD_WIDTH)  1.61 us

profile of v1, /device:TPU:0, one launch (start us, length us, event | category | flops | bytes accessed | tf_op | source)
XLA Modules:
  0.0 49.1 jit_solution(10628732093347783573)
XLA Ops:
  0.0 0.1 pad_maximum_fusion
  0.1 0.6 %broadcast_in_dim.2.freq_ref = f32[8,128]{1,0:T(8,128)} broadcast(f32[128]{0:T(128)S(1)} %pad_maximum_fusion), dimensions={1} | broadcast | bytes 4608 | tf_op jit(solution)/shard_map/broadcast_in_dim | solution.py:317
  0.7 46.8 %shard_map.73 = bf16[512,128]{1,0:T(8,128)(2,1)} custom-call(bf16[8,8192]{1,0:T(8,128)(2,1)} %x_ref.1, bf16[8192,2048]{1,0:T(8,128)(2,1)} %wq_ref.1, bf16[8192,256]{1,0:T(8,128)(2,1)} %wkv_ref.1, bf16[4,192,1024]{2,1,0:T(8,128)(2,1)} %keys_ref.1, bf16[4,192,1024]{2,1,0:T(8,128)(2,1)} %values_ref.1, s32[4]{0:T(128)} %lengths_ref.1, s32[4]{0:T(128)} %positions_ref.1, ...), custom_call_target="tpu_custom_call" | custom-call | tf_op jit(solution)/shard_map/pallas_call | solution.py:320
  47.5 1.6 %reshape.4 = bf16[4,16384]{1,0:T(4,128)(2,1)} reshape(bf16[512,128]{1,0:T(8,128)(2,1)} %shard_map.73) | data formatting | bytes 262144 | tf_op jit(solution)/shard_map/reshape | solution.py:350
  (1 shorter events, 0.0 us)

commit v2 on v1

--- a/solution.py
+++ b/solution.py
@@ -103,7 +103,9 @@
 WIDE = 8
 GROUP = 16
 HEADS = GROUP + 2
-CHUNKS = 4
+CUTS = (0, 8, 16, 24, 32)
+CHUNKS = len(CUTS) - 1
+TILE = 512
 ROWS = 4
 SLOTS = 192
 PACK = 80
@@ -111,9 +113,9 @@
 
 
 def kernel(
-    x_ref, wq_ref, wkv_ref, keys_ref, values_ref, lengths_ref, positions_ref, freq_ref, out_ref,
+    x_ref, wq_ref, wkv_ref, keys_ref, values_ref, lengths_ref, positions_ref, out_ref,
     gathered, wq, wkv, keys, values, left, acc, give, take, spread, parcel, landed, sums,
-    sum_send, sum_recv, own_send, fwd_send, gather_recv, wq_sem, wkv_sem, key_sem, value_sem,
+    sum_send, sum_recv, own_send, across_send, gather_recv, weight_sem, key_sem, value_sem,
     give_send, give_recv, parcel_send, parcel_recv,
 ):
     me = lax.axis_index("wide")
@@ -121,14 +123,21 @@
     other = 1 - core
     peer = me + 1 - 2 * lax.rem(me, 2)
     features = x_ref.shape[1]
-    width = features // CHUNKS
-    half = width // 2
-
-    def wq_copy(c):
-        return pltpu.make_async_copy(wq_ref.at[pl.ds(c * width, width)], wq.at[c], wq_sem.at[c])
-
-    def wkv_copy(c):
-        return pltpu.make_async_copy(wkv_ref.at[pl.ds(c * width, width)], wkv.at[c], wkv_sem.at[c])
+    half = features // 2
+    cuts = [half // CUTS[-1] * cut for cut in CUTS]
+
+    def span(c):
+        return pl.ds(cuts[c], cuts[c + 1] - cuts[c])
+
+    def lower(c):
+        return pl.ds(half + cuts[c], cuts[c + 1] - cuts[c])
+
+    def weight_copies(c):
+        return [
+            pltpu.make_async_copy(source.at[rows], kept.at[rows], weight_sem.at[c, i, j])
+            for i, (source, kept) in enumerate(((wq_ref, wq), (wkv_ref, wkv)))
+            for j, rows in enumerate((span(c), lower(c)))
+        ]
 
     key_copy = pltpu.make_async_copy(keys_ref, keys, key_sem)
     value_copy = pltpu.make_async_copy(values_ref, values, value_sem)
@@ -141,8 +150,8 @@
     pl.semaphore_signal(barrier, inc=1, device_id={"narrow": other}, device_id_type=MESH)
 
     for c in range(CHUNKS):
-        wq_copy(c).start()
-        wkv_copy(c).start()
+        for copy in weight_copies(c):
+            copy.start()
     key_copy.start()
     value_copy.start()
 
@@ -161,71 +170,82 @@
 
     def send(c, slot, target, sem):
         return pltpu.make_async_remote_copy(
-            src_ref=gathered.at[c, slot], dst_ref=gathered.at[c, slot], send_sem=sem,
+            src_ref=gathered.at[slot, :, span(c)], dst_ref=gathered.at[slot, :, span(c)], send_sem=sem,
             recv_sem=gather_recv.at[c, slot], device_id={"wide": target}, device_id_type=MESH,
         )
 
+    def across(c, slot):
+        return send(c, slot, peer, across_send.at[c, slot])
+
     def along(c, d):
         return send(c, me, lax.rem(me + 2 * d, WIDE), own_send.at[c, d])
 
-    def across(c):
-        return send(c, me, peer, own_send.at[c, 0])
-
-    def forward(c, d):
-        return send(c, lax.rem(me + 2 * d, WIDE), peer, fwd_send.at[c, d])
-
-    for c in range(CHUNKS):
-        first = x_ref[:, c * width : c * width + half].astype(jnp.float32) * scale
-        second = x_ref[:, c * width + half : (c + 1) * width].astype(jnp.float32) * scale
-        gathered[c, me] = jnp.concatenate([first, second], axis=0).astype(jnp.bfloat16)
+    def relay(c, d):
+        slot = lax.rem(me + 2 * d, WIDE)
+        across(c, slot).wait_recv()
+        across(c, slot).start()
+
+    def originate(c):
+        first = x_ref[:, span(c)].astype(jnp.float32) * scale
+        second = x_ref[:, lower(c)].astype(jnp.float32) * scale
+        gathered[me, :, span(c)] = jnp.concatenate([first, second], axis=0).astype(jnp.bfloat16)
         for d in range(1, 4):
             along(c, d).start()
-        across(c).start()
-
-    angles = [positions_ref[r].astype(jnp.float32) * freq_ref[0:1, :] for r in range(ROWS)]
-    cosine = [jnp.cos(a) for a in angles]
-    sign = jnp.where(lax.broadcasted_iota(jnp.int32, (1, HEAD_WIDTH), 1) < HEAD_WIDTH // 2, -1.0, 1.0)
-    sine = [jnp.sin(a) * sign for a in angles]
-
-    def pass_on(c):
-        for d in (1, 3, 2):
-            slot = lax.rem(me + 2 * d, WIDE)
-            send(c, slot, peer, fwd_send.at[c, d]).wait_recv()
-            forward(c, d).start()
-
-    pass_on(0)
-    for c in range(CHUNKS):
-        if c + 1 < CHUNKS:
-            pass_on(c + 1)
-        for d in range(4):
-            slot = lax.rem(peer + 2 * d, WIDE)
-            send(c, slot, peer, fwd_send.at[c, 0]).wait_recv()
-        block = gathered[c].astype(jnp.float32)
-        left[:, :half] = block[:, :8].reshape(8 * WIDE, half).astype(jnp.bfloat16)
-        left[:, half:] = block[:, 8:].reshape(8 * WIDE, half).astype(jnp.bfloat16)
-        wq_copy(c).wait()
-        wkv_copy(c).wait()
-
-        def accumulate(j, product):
-            for i in range(2):
-                at = pl.ds(pl.multiple_of((2 * j + i) * 64, 64), 64)
+        across(c, me).start()
+
+    def multiply(c, between):
+        for level_at in range(WIDE // 2):
+            across(c, 2 * level_at + lax.rem(peer, 2)).wait_recv()
+        block = gathered[:, :, span(c)].astype(jnp.float32)
+        size = cuts[c + 1] - cuts[c]
+        left[:, span(c)] = block[:, :8].reshape(8 * WIDE, size).astype(jnp.bfloat16)
+        left[:, lower(c)] = block[:, 8:].reshape(8 * WIDE, size).astype(jnp.bfloat16)
+        for copy in weight_copies(c):
+            copy.wait()
+
+        def accumulate(start, columns, kept):
+            product = jnp.dot(
+                left[:, span(c)], kept[span(c), columns], preferred_element_type=jnp.float32
+            ) + jnp.dot(
+                left[:, lower(c)], kept[lower(c), columns], preferred_element_type=jnp.float32
+            )
+            for i in range(product.shape[1] // 128):
+                at = pl.ds(start + i * 64, 64)
                 piece = product[:, i * 128 : (i + 1) * 128]
                 if c == 0:
                     acc[at, :] = piece
                 else:
                     acc[at, :] += piece
 
-        def tile(j, carry):
-            columns = pl.ds(pl.multiple_of(j * 256, 256), 256)
-            accumulate(
-                j, jnp.dot(left[...], wq[c, :, columns], preferred_element_type=jnp.float32)
-            )
-            return carry
-
-        lax.fori_loop(0, GROUP // 2, tile, 0)
-        accumulate(
-            GROUP // 2, jnp.dot(left[...], wkv[c], preferred_element_type=jnp.float32)
-        )
+        tiles = GROUP * HEAD_WIDTH // TILE
+        for j in range(tiles):
+            accumulate(j * TILE // 2, pl.ds(j * TILE, TILE), wq)
+            if j < len(between):
+                between[j]()
+        for step in between[tiles:]:
+            step()
+        accumulate(GROUP * 64, pl.ds(0, 2 * HEAD_WIDTH), wkv)
+
+    def ahead(c, d):
+        if c < CHUNKS:
+            relay(c, d)
+
+    for c in range(CHUNKS):
+        originate(c)
+    lane = lax.broadcasted_iota(jnp.int32, (1, HEAD_WIDTH), 1)
+    frequency = jnp.ones((1, HEAD_WIDTH), jnp.float32)
+    for bit in range(6):
+        factor = float(np.float32(500000.0 ** (-(2.0**bit) / 64)))
+        frequency = frequency * jnp.where((lane // 2**bit) % 2 == 1, factor, 1.0)
+    angles = [positions_ref[r].astype(jnp.float32) * frequency for r in range(ROWS)]
+    cosine = [jnp.cos(a) for a in angles]
+    sign = jnp.where(lane < HEAD_WIDTH // 2, -1.0, 1.0)
+    sine = [jnp.sin(a) * sign for a in angles]
+    for c in range(2):
+        for d in (1, 3, 2):
+            relay(c, d)
+    for c in range(CHUNKS):
+        multiply(c, [functools.partial(ahead, c + 2, d) for d in (1, 3, 2)])
 
     for h in range(HEADS):
         for r in range(ROWS):
@@ -268,42 +288,66 @@
         ).wait_recv()
 
     scaling = HEAD_WIDTH ** (-0.5)
-    slot_index = lax.broadcasted_iota(jnp.int32, (GROUP, SLOTS), 1)
+    slot_index = lax.broadcasted_iota(jnp.int32, (WIDE * GROUP, SLOTS), 1)
+    none = jnp.zeros((GROUP, HEAD_WIDTH), jnp.bfloat16)
+    pair = landed[:, 64:PACK, :].astype(jnp.float32)
 
     def rotated(v, r):
         return (v * cosine[r] + pltpu.roll(v, HEAD_WIDTH // 2, 1) * sine[r]).astype(jnp.bfloat16)
 
+    def wide(start):
+        return slice(start * 2 * HEAD_WIDTH, (start + 1) * 2 * HEAD_WIDTH)
+
+    queries, owns, new_values, scores = [], [], [], []
+    for r in range(ROWS):
+        raw = landed[:, r * GROUP : (r + 1) * GROUP, :].astype(jnp.float32)
+        query = rotated(raw.reshape(WIDE * GROUP, HEAD_WIDTH), r)
+        new_key = pair[:, 2 * r : 2 * r + 1, :].reshape(WIDE, HEAD_WIDTH)
+        new_key = rotated(new_key, r).astype(jnp.float32).reshape(WIDE, 1, HEAD_WIDTH)
+        grouped = query.astype(jnp.float32).reshape(WIDE, GROUP, HEAD_WIDTH)
+        own = jnp.sum(grouped * new_key, axis=2, keepdims=True) * scaling
+        owns.append(own.reshape(WIDE * GROUP, 1))
+        new_values.append(pair[:, 2 * r + 1 : 2 * r + 2, :])
+        parts = []
+        for p in range(WIDE // 2):
+            even = query[2 * p * GROUP : (2 * p + 1) * GROUP]
+            odd = query[(2 * p + 1) * GROUP : (2 * p + 2) * GROUP]
+            both = jnp.concatenate(
+                [jnp.concatenate([even, none], axis=1), jnp.concatenate([none, odd], axis=1)], axis=0
+            )
+            parts.append(
+                lax.dot_general(
+                    both, keys[r, :, wide(p)], (((1,), (1,)), ((), ())),
+                    preferred_element_type=jnp.float32,
+                )
+            )
+        scores.append(jnp.concatenate(parts, axis=0) * scaling)
     for r in range(ROWS):
         live = slot_index < lengths_ref[r]
-        for g in range(WIDE):
-            columns = slice(g * HEAD_WIDTH, (g + 1) * HEAD_WIDTH)
-            query = rotated(landed[g, r * GROUP : (r + 1) * GROUP, :].astype(jnp.float32), r)
-            pair = landed[g, 64:PACK, :].astype(jnp.float32)
-            new_key = rotated(pair, r)[2 * r : 2 * r + 1].astype(jnp.float32)
-            new_value = pair[2 * r + 1 : 2 * r + 2]
-            own = jnp.sum(query.astype(jnp.float32) * new_key, axis=1, keepdims=True) * scaling
-            scores = lax.dot_general(
-                query, keys[r, :, columns], (((1,), (1,)), ((), ())),
-                preferred_element_type=jnp.float32,
-            ) * scaling
-            masked = jnp.where(live, scores, -1e30)
-            peak = jnp.maximum(jnp.max(masked, axis=1, keepdims=True), own)
-            weights = jnp.where(live, jnp.exp(masked - peak), 0.0)
-            own_weight = jnp.exp(own - peak)
-            totals = jnp.sum(weights, axis=1, keepdims=True) + own_weight
-            blended = jnp.dot(
-                weights.astype(jnp.bfloat16), values[r, :, columns],
+        masked = jnp.where(live, scores[r], -1e30)
+        peak = jnp.maximum(jnp.max(masked, axis=1, keepdims=True), owns[r])
+        weights = jnp.where(live, jnp.exp(masked - peak), 0.0)
+        own_weight = jnp.exp(owns[r] - peak)
+        totals = jnp.sum(weights, axis=1, keepdims=True) + own_weight
+        rounded = weights.astype(jnp.bfloat16)
+        parts = []
+        for p in range(WIDE // 2):
+            both = jnp.dot(
+                rounded[2 * p * GROUP : (2 * p + 2) * GROUP], values[r, :, wide(p)],
                 preferred_element_type=jnp.float32,
             )
-            blended = blended + own_weight.astype(jnp.bfloat16).astype(jnp.float32) * new_value
-            at = r * WIDE * GROUP + g * GROUP
-            out_ref[at : at + GROUP, :] = (blended / totals).astype(jnp.bfloat16)
+            parts += [both[:GROUP, :HEAD_WIDTH], both[GROUP:, HEAD_WIDTH:]]
+        own_rounded = own_weight.astype(jnp.bfloat16).astype(jnp.float32)
+        added = own_rounded.reshape(WIDE, GROUP, 1) * new_values[r]
+        blended = jnp.concatenate(parts, axis=0) + added.reshape(WIDE * GROUP, HEAD_WIDTH)
+        at = r * WIDE * GROUP
+        out_ref[at : at + WIDE * GROUP, :] = (blended * (1.0 / totals)).astype(jnp.bfloat16)
 
     for c in range(CHUNKS):
+        for k in range(WIDE // 2):
+            across(c, 2 * k + lax.rem(me, 2)).wait_send()
         for d in range(1, 4):
             along(c, d).wait_send()
-            forward(c, d).wait_send()
-        across(c).wait_send()
     for d in range(1, WIDE):
         deliver(d).wait_send()
 
@@ -312,23 +356,20 @@
     hidden_rows, query_weight, key_value_weight, cache_keys, earlier_values, lengths, positions
 ):
     features = hidden_rows.shape[1]
-    width = features // CHUNKS
-    frequency = 500000.0 ** (-(jnp.arange(HEAD_WIDTH // 2).astype(jnp.float32) * 2.0 / HEAD_WIDTH))
-    frequency = jnp.broadcast_to(jnp.concatenate([frequency, frequency])[None], (8, HEAD_WIDTH))
     dma = pltpu.SemaphoreType.DMA
     vmem, anywhere, smem = (pl.BlockSpec(memory_space=s) for s in (pltpu.VMEM, pl.ANY, pltpu.SMEM))
     result = pl.pallas_call(
         kernel,
         out_shape=jax.ShapeDtypeStruct((ROWS * WIDE * GROUP, HEAD_WIDTH), jnp.bfloat16),
-        in_specs=[vmem, anywhere, anywhere, anywhere, anywhere, smem, smem, vmem],
+        in_specs=[vmem, anywhere, anywhere, anywhere, anywhere, smem, smem],
         out_specs=vmem,
         scratch_shapes=[
-            pltpu.VMEM((CHUNKS, WIDE, 16, width // 2), jnp.bfloat16),
-            pltpu.VMEM((CHUNKS, width, GROUP * HEAD_WIDTH), jnp.bfloat16),
-            pltpu.VMEM((CHUNKS, width, 2 * HEAD_WIDTH), jnp.bfloat16),
+            pltpu.VMEM((WIDE, 16, features // 2), jnp.bfloat16),
+            pltpu.VMEM((features, GROUP * HEAD_WIDTH), jnp.bfloat16),
+            pltpu.VMEM((features, 2 * HEAD_WIDTH), jnp.bfloat16),
             pltpu.VMEM((ROWS, SLOTS, WIDE * HEAD_WIDTH), jnp.bfloat16),
             pltpu.VMEM((ROWS, SLOTS, WIDE * HEAD_WIDTH), jnp.bfloat16),
-            pltpu.VMEM((8 * WIDE, width), jnp.bfloat16),
+            pltpu.VMEM((8 * WIDE, features), jnp.bfloat16),
             pltpu.VMEM((HEADS * 64, HEAD_WIDTH), jnp.float32),
             pltpu.VMEM((HEADS * 32, HEAD_WIDTH), jnp.float32),
             pltpu.VMEM((HEADS * 32, HEAD_WIDTH), jnp.float32),
@@ -336,8 +377,8 @@
             pltpu.VMEM((WIDE, PACK, HEAD_WIDTH), jnp.bfloat16),
             pltpu.VMEM((WIDE, PACK, HEAD_WIDTH), jnp.bfloat16),
             pltpu.VMEM((2, 8, 128), jnp.float32),
-            dma, dma, dma((CHUNKS, 4)), dma((CHUNKS, 4)), dma((CHUNKS, WIDE)),
-            dma((CHUNKS,)), dma((CHUNKS,)), dma, dma,
+            dma, dma, dma((CHUNKS, 4)), dma((CHUNKS, WIDE)), dma((CHUNKS, WIDE)),
+            dma((CHUNKS, 2, 2)), dma, dma,
             dma, dma, dma((WIDE,)), dma((WIDE,)),
         ],
         compiler_params=pltpu.CompilerParams(
@@ -345,7 +386,7 @@
         ),
     )(
         hidden_rows, query_weight, key_value_weight, cache_keys, earlier_values, lengths,
-        positions, frequency,
+        positions,
     )
     return result.reshape(ROWS, WIDE * GROUP * HEAD_WIDTH)
 

time: 49.3 us -> 39.5 us (0.80)
  Pallas kernels: 46.8 us -> 37.7 us
  local copies, waits for them, and re-layouts: 2.21 us -> 1.61 us
    pallas_call x1, Pallas kernels: 46.8 us -> 37.7 us  [fused(): pl.pallas_call(kernel, out_shape=jax.ShapeDtypeStruct((ROWS * WIDE * GROU...]
    broadcast_in_dim x1 -> x0, local copies, waits for them, and re-layouts: 0.6 us -> none  [fused(): jnp.broadcast_to(jnp.concatenate([frequency, frequency])[None], (8, HEAD_...]
where the time goes in v2:
time: 39.5 us; the launch traced here: 39.3 us
  Pallas kernels  37.7 us (95%)
  local copies, waits for them, and re-layouts  1.61 us (4%)
    pallas_call x1, Pallas kernels, fused(): pl.pallas_call(kernel, out_shape=jax.ShapeDtypeStruct((ROWS * WIDE * GROU...  37.7 us
    reshape x1, local copies, waits for them, and re-layouts, fused(): return result.reshape(ROWS, WIDE * GROUP * HEAD_WIDTH)  1.61 us

profile of v2, /device:TPU:0, one launch (start us, length us, event | category | flops | bytes accessed | tf_op | source)
XLA Modules:
  0.0 39.3 jit_solution(16695174040751722598)
XLA Ops:
  0.0 37.7 %shard_map.73 = bf16[512,128]{1,0:T(8,128)(2,1)} custom-call(bf16[8,8192]{1,0:T(8,128)(2,1)} %x_ref.1, bf16[8192,2048]{1,0:T(8,128)(2,1)} %wq_ref.1, bf16[8192,256]{1,0:T(8,128)(2,1)} %wkv_ref.1, bf16[4,192,1024]{2,1,0:T(8,128)(2,1)} %keys_ref.1, bf16[4,192,1024]{2,1,0:T(8,128)(2,1)} %values_ref.1, s32[4]{0:T(128)} %lengths_ref.1, s32[4]{0:T(128)} %positions_ref.1), custom_call_target="tpu_custom_call" | custom-call | tf_op jit(solution)/shard_map/pallas_call | solution.py:361
  37.7 1.6 %reshape.3 = bf16[4,16384]{1,0:T(4,128)(2,1)} reshape(bf16[512,128]{1,0:T(8,128)(2,1)} %shard_map.73) | data formatting | bytes 262144 | tf_op jit(solution)/shard_map/reshape | solution.py:391

commit v3 on v2

--- a/solution.py
+++ b/solution.py
@@ -109,12 +109,14 @@
 ROWS = 4
 SLOTS = 192
 PACK = 80
+PARTS = ((0, 32), (32, PACK))
+HALVES = ((0, 8), (8, HEADS))
 MESH = pl.DeviceIdType.MESH
 
 
 def kernel(
     x_ref, wq_ref, wkv_ref, keys_ref, values_ref, lengths_ref, positions_ref, out_ref,
-    gathered, wq, wkv, keys, values, left, acc, give, take, spread, parcel, landed, sums,
+    gathered, wq, wkv, keys, values, left, acc, give, take, spread, parcel, landed, sums, final,
     sum_send, sum_recv, own_send, across_send, gather_recv, weight_sem, key_sem, value_sem,
     give_send, give_recv, parcel_send, parcel_recv,
 ):
@@ -244,53 +246,67 @@
     for c in range(2):
         for d in (1, 3, 2):
             relay(c, d)
-    for c in range(CHUNKS):
-        multiply(c, [functools.partial(ahead, c + 2, d) for d in (1, 3, 2)])
-
-    for h in range(HEADS):
-        for r in range(ROWS):
-            give[pl.ds(h * 32 + r * 8, 8), :] = acc[pl.ds(h * 64 + other * 4 + r, 8, stride=8), :]
-    trade = pltpu.make_async_remote_copy(
-        src_ref=give, dst_ref=take, send_sem=give_send, recv_sem=give_recv,
-        device_id={"narrow": other}, device_id_type=MESH,
-    )
-    trade.start()
+    def trade(p):
+        rows = pl.ds(HALVES[p][0] * 32, (HALVES[p][1] - HALVES[p][0]) * 32)
+        return pltpu.make_async_remote_copy(
+            src_ref=give.at[rows], dst_ref=take.at[rows], send_sem=give_send.at[p],
+            recv_sem=give_recv.at[p], device_id={"narrow": other}, device_id_type=MESH,
+        )
+
+    def offer(p):
+        for h in range(*HALVES[p]):
+            for r in range(ROWS):
+                kept = acc[pl.ds(h * 64 + other * 4 + r, 8, stride=8), :]
+                give[pl.ds(h * 32 + r * 8, 8), :] = kept
+        trade(p).start()
+
+    def deliver(d, p, slot):
+        target = lax.rem(me + d, WIDE)
+        rows = pl.ds(PARTS[p][0], PARTS[p][1] - PARTS[p][0])
+        return pltpu.make_async_remote_copy(
+            src_ref=parcel.at[target, rows], dst_ref=landed.at[slot, rows],
+            send_sem=parcel_send.at[target, p], recv_sem=parcel_recv.at[slot, p],
+            device_id={"wide": target}, device_id_type=MESH,
+        )
+
+    def dispatch(p):
+        trade(p).wait()
+        start, stop = PARTS[p]
+        for h in range(*HALVES[p]):
+            for r in range(ROWS):
+                total = (
+                    acc[pl.ds(h * 64 + core * 4 + r, 8, stride=8), :]
+                    + take[pl.ds(h * 32 + r * 8, 8), :]
+                )
+                row = h // 8 * 32 + r * 8 + h % 8 if h < GROUP else 64 + 2 * r + h - GROUP
+                spread[pl.ds(row, 8, stride=PACK), :] = total
+        for w in range(WIDE):
+            parcel[w, start:stop, :] = spread[w * PACK + start : w * PACK + stop, :].astype(
+                jnp.bfloat16
+            )
+        for d in (4, 3, 5, 2, 6, 1, 7):
+            deliver(d, p, me).start()
+        landed[me, start:stop, :] = parcel[me, start:stop, :]
+
     for w in range(WIDE):
         spread[pl.ds(w * PACK + 72, 8), :] = jnp.zeros((8, HEAD_WIDTH), jnp.float32)
-    trade.wait()
-    for h in range(HEADS):
-        for r in range(ROWS):
-            total = (
-                acc[pl.ds(h * 64 + core * 4 + r, 8, stride=8), :]
-                + take[pl.ds(h * 32 + r * 8, 8), :]
-            )
-            row = r * GROUP + h if h < GROUP else 64 + 2 * r + h - GROUP
-            spread[pl.ds(row, 8, stride=PACK), :] = total
-
-    def deliver(d):
-        target = lax.rem(me + d, WIDE)
-        return pltpu.make_async_remote_copy(
-            src_ref=parcel.at[target], dst_ref=landed.at[me], send_sem=parcel_send.at[target],
-            recv_sem=parcel_recv.at[me], device_id={"wide": target}, device_id_type=MESH,
-        )
-
-    parcel[...] = spread[...].astype(jnp.bfloat16).reshape(WIDE, PACK, HEAD_WIDTH)
-    for d in (4, 3, 5, 2, 6, 1, 7):
-        deliver(d).start()
-    landed[me] = parcel[me]
+    for c in range(CHUNKS - 1):
+        multiply(c, [functools.partial(ahead, c + 2, d) for d in (1, 3, 2)])
+    multiply(CHUNKS - 1, [lambda: None, lambda: offer(0), lambda: None, lambda: dispatch(0)])
+    offer(1)
+    dispatch(1)
     key_copy.wait()
     value_copy.wait()
-    for d in range(1, WIDE):
-        source = lax.rem(me + d, WIDE)
-        pltpu.make_async_remote_copy(
-            src_ref=parcel.at[source], dst_ref=landed.at[source], send_sem=parcel_send.at[source],
-            recv_sem=parcel_recv.at[source], device_id={"wide": source}, device_id_type=MESH,
-        ).wait_recv()
+    for p in range(2):
+        for d in range(1, WIDE):
+            deliver(d, p, lax.rem(me + d, WIDE)).wait_recv()
 
     scaling = HEAD_WIDTH ** (-0.5)
     slot_index = lax.broadcasted_iota(jnp.int32, (WIDE * GROUP, SLOTS), 1)
     none = jnp.zeros((GROUP, HEAD_WIDTH), jnp.bfloat16)
     pair = landed[:, 64:PACK, :].astype(jnp.float32)
+    early = landed[:, :32, :].astype(jnp.float32)
+    later = landed[:, 32:64, :].astype(jnp.float32)
 
     def rotated(v, r):
         return (v * cosine[r] + pltpu.roll(v, HEAD_WIDTH // 2, 1) * sine[r]).astype(jnp.bfloat16)
@@ -300,7 +316,9 @@
 
     queries, owns, new_values, scores = [], [], [], []
     for r in range(ROWS):
-        raw = landed[:, r * GROUP : (r + 1) * GROUP, :].astype(jnp.float32)
+        raw = jnp.concatenate(
+            [early[:, r * 8 : (r + 1) * 8, :], later[:, r * 8 : (r + 1) * 8, :]], axis=1
+        )
         query = rotated(raw.reshape(WIDE * GROUP, HEAD_WIDTH), r)
         new_key = pair[:, 2 * r : 2 * r + 1, :].reshape(WIDE, HEAD_WIDTH)
         new_key = rotated(new_key, r).astype(jnp.float32).reshape(WIDE, 1, HEAD_WIDTH)
@@ -341,15 +359,20 @@
         added = own_rounded.reshape(WIDE, GROUP, 1) * new_values[r]
         blended = jnp.concatenate(parts, axis=0) + added.reshape(WIDE * GROUP, HEAD_WIDTH)
         at = r * WIDE * GROUP
-        out_ref[at : at + WIDE * GROUP, :] = (blended * (1.0 / totals)).astype(jnp.bfloat16)
+        final[at : at + WIDE * GROUP, :] = blended * (1.0 / totals)
+
+    for h in range(WIDE * GROUP):
+        rows = final[pl.ds(h, ROWS, stride=WIDE * GROUP), :]
+        out_ref[:, h * HEAD_WIDTH : (h + 1) * HEAD_WIDTH] = rows.astype(jnp.bfloat16)
 
     for c in range(CHUNKS):
         for k in range(WIDE // 2):
             across(c, 2 * k + lax.rem(me, 2)).wait_send()
         for d in range(1, 4):
             along(c, d).wait_send()
-    for d in range(1, WIDE):
-        deliver(d).wait_send()
+    for p in range(2):
+        for d in range(1, WIDE):
+            deliver(d, p, me).wait_send()
 
 
 def fused(
@@ -358,9 +381,9 @@
     features = hidden_rows.shape[1]
     dma = pltpu.SemaphoreType.DMA
     vmem, anywhere, smem = (pl.BlockSpec(memory_space=s) for s in (pltpu.VMEM, pl.ANY, pltpu.SMEM))
-    result = pl.pallas_call(
+    return pl.pallas_call(
         kernel,
-        out_shape=jax.ShapeDtypeStruct((ROWS * WIDE * GROUP, HEAD_WIDTH), jnp.bfloat16),
+        out_shape=jax.ShapeDtypeStruct((ROWS, WIDE * GROUP * HEAD_WIDTH), jnp.bfloat16),
         in_specs=[vmem, anywhere, anywhere, anywhere, anywhere, smem, smem],
         out_specs=vmem,
         scratch_shapes=[
@@ -377,9 +400,10 @@
             pltpu.VMEM((WIDE, PACK, HEAD_WIDTH), jnp.bfloat16),
             pltpu.VMEM((WIDE, PACK, HEAD_WIDTH), jnp.bfloat16),
             pltpu.VMEM((2, 8, 128), jnp.float32),
+            pltpu.VMEM((ROWS * WIDE * GROUP, HEAD_WIDTH), jnp.float32),
             dma, dma, dma((CHUNKS, 4)), dma((CHUNKS, WIDE)), dma((CHUNKS, WIDE)),
             dma((CHUNKS, 2, 2)), dma, dma,
-            dma, dma, dma((WIDE,)), dma((WIDE,)),
+            dma((2,)), dma((2,)), dma((WIDE, 2)), dma((WIDE, 2)),
         ],
         compiler_params=pltpu.CompilerParams(
             collective_id=0, has_side_effects=True, vmem_limit_bytes=56 * 1024 * 1024
@@ -388,7 +412,6 @@
         hidden_rows, query_weight, key_value_weight, cache_keys, earlier_values, lengths,
         positions,
     )
-    return result.reshape(ROWS, WIDE * GROUP * HEAD_WIDTH)
 
 
 def solution(mesh):

time: 39.5 us -> 39 us (0.987)
  Pallas kernels: 37.7 us -> 37.2 us
    unnamed x0 -> x1, local copies, waits for them, and re-layouts: none -> 1.61 us
    reshape x1 -> x0, local copies, waits for them, and re-layouts: 1.61 us -> none  [fused(): return result.reshape(ROWS, WIDE * GROUP * HEAD_WIDTH)]
    pallas_call x1, Pallas kernels: 37.7 us -> 37.2 us  [fused(): pl.pallas_call(kernel, out_shape=jax.ShapeDtypeStruct((ROWS, WIDE * GROUP...]
where the time goes in v3:
time: 39 us; the launch traced here: 38.8 us
  Pallas kernels  37.2 us (95%)
  local copies, waits for them, and re-layouts  1.61 us (4%)
    pallas_call x1, Pallas kernels, fused(): pl.pallas_call(kernel, out_shape=jax.ShapeDtypeStruct((ROWS, WIDE * GROUP...  37.2 us
    unnamed x1, local copies, waits for them, and re-layouts  1.61 us

profile of v3, /device:TPU:0, one launch (start us, length us, event | category | flops | bytes accessed | tf_op | source)
XLA Modules:
  0.0 38.8 jit_solution(8775497491146871728)
XLA Ops:
  0.0 37.2 %shard_map.73 = bf16[4,16384]{1,0:T(4,128)(2,1)} custom-call(bf16[8,8192]{1,0:T(8,128)(2,1)} %x_ref.1, bf16[8192,2048]{1,0:T(8,128)(2,1)} %wq_ref.1, bf16[8192,256]{1,0:T(8,128)(2,1)} %wkv_ref.1, bf16[4,192,1024]{2,1,0:T(8,128)(2,1)} %keys_ref.1, bf16[4,192,1024]{2,1,0:T(8,128)(2,1)} %values_ref.1, s32[4]{0:T(128)} %lengths_ref.1, s32[4]{0:T(128)} %positions_ref.1), custom_call_target="tpu_custom_call" | custom-call | tf_op jit(solution)/shard_map/pallas_call | solution.py:384
  37.2 1.6 %copy.9 = bf16[4,16384]{1,0:T(4,128)(2,1)} copy(bf16[4,16384]{1,0:T(4,128)(2,1)} %shard_map.73) | data formatting | bytes 262144
